TPU v7x, 32 devices: a whole 2x2x4 slice. The times are simulated.
32 devices in a mesh: dp: 4 (over y, x), row: 2 (over core), col: 4 (over z).
Axes of the slice: x: 2, y: 2, z: 4, core: 2. Of those that a mesh axis runs over, the one named last changes fastest.
Arguments:
- attn_heads: bfloat16 [12288, 2304], P(('dp', 'col'), 'row'), may hold values from -6 to 6
- out_weight: bfloat16 [2304, 4096], P('row', 'col'), may hold values from -0.125 to 0.125
- cotangent: bfloat16 [12288, 4096], P(('dp', 'row'), 'col'), may hold values from -6 to 6
Outputs:
- head_grad: bfloat16 [12288, 2304], P(('dp', 'col'), 'row')
- weight_grad: float32 [2304, 4096], P('row', 'col')
All inputs are finite; a program needn't handle non-finite values.
Results may differ from a plain program's by a relative error of at most 0.015.
Values may be sent and summed in bfloat16 or wider, within the bound.
A program may use at most 64 MiB of HBM per device.

v0:
```python
import jax
import jax.numpy as jnp
from jax import lax
from jax.sharding import PartitionSpec as P


def per_device(attn_heads, out_weight, cotangent):
    heads_all = lax.all_gather(attn_heads, "col", axis=0, tiled=True)
    cot_all = lax.all_gather(cotangent, "row", axis=0, tiled=True)
    tok_replica = cot_all.shape[0]
    grad_scale = float(tok_replica * lax.axis_size("dp")) ** (-0.5)
    summed = lax.psum_scatter(
        lax.dot_general(
            cot_all, out_weight, (((1,), (1,)), ((), ())), preferred_element_type=jnp.float32
        ).astype(jnp.bfloat16),
        "col",
        scatter_dimension=0,
        tiled=True,
    )
    weight_grad = (
        lax.psum(
            lax.dot_general(
                heads_all, cot_all, (((0,), (0,)), ((), ())), preferred_element_type=jnp.float32
            ).astype(jnp.bfloat16),
            "dp",
        ).astype(jnp.float32)
        * grad_scale
    )
    return (summed, weight_grad)


def solution(mesh):
    return jax.shard_map(
        per_device,
        mesh=mesh,
        in_specs=(P(("dp", "col"), "row"), P("row", "col"), P(("dp", "row"), "col")),
        out_specs=(P(("dp", "col"), "row"), P("row", "col")),
        check_vma=False,
    )
```

profile of v0, /device:TPU:0, one launch (start us, length us, event | category | flops | bytes accessed | tf_op | source)
XLA Modules:
  0.0 378.1 jit_solution(17359295000872395346)
XLA Ops:
  7.2 0.0 copy-start
  7.2 0.0 all-gather.3.cloned.1.call-start
  7.2 0.7 all-gather.3.cloned.1.call-update
  7.9 0.0 all-gather.5.cloned.1.call-start
  8.0 0.7 all-gather.5.cloned.1.call-update
  8.7 0.0 all-reduce.2.cloned.1.call-start
  8.7 20.3 %all-gather.3.cloned.1.call-done = bf16[3072,1024]{1,0:T(8,128)(2,1)} async-done(((bf16[1536,1024]{1,0:T(8,128)(2,1)}), bf16[3072,1024]{1,0:T(8,128)(2,1)}) %all-gather.3.cloned.1.call-update) | async-done | bytes 6291472 | tf_op jit(solution)/shard_map/all_gather | solution.py:9
  29.0 131.0 %all-gather.5.cloned.1.call-done = bf16[3072,1152]{1,0:T(8,128)(2,1)} async-done(((bf16[768,1152]{1,0:T(8,128)(2,1)}), bf16[3072,1152]{1,0:T(8,128)(2,1)}) %all-gather.5.cloned.1.call-update) | async-done | bytes 7077904 | tf_op jit(solution)/shard_map/all_gather | solution.py:8
  160.0 12.7 %convolution_convert_fusion.1 = bf16[1152,1024]{1,0:T(8,128)(2,1)} fusion(bf16[3072,1152]{1,0:T(8,128)(2,1)} %all-gather.5.cloned.1.call-done, bf16[3072,1024]{1,0:T(8,128)(2,1)} %all-gather.3.cloned.1.call-done), kind=kOutput, calls=%fused_computation.2 | convolution fusion | flops 7248936960 | bytes 15728640 | tf_op jit(solution)/shard_map/dot_general | solution.py:22
  172.8 0.0 all-reduce.2.cloned.1.call-update
  172.8 0.0 reduce-scatter.2.cloned.1.call-start
  172.8 0.0 copy-done
  172.9 12.3 %convolution_convert_fusion = bf16[3072,1152]{1,0:T(8,128)(2,1)} fusion(bf16[3072,1024]{1,0:T(8,128)(2,1)} %all-gather.3.cloned.1.call-done, bf16[1152,1024]{1,0:T(8,128)(2,1)S(1)} %copy-done), kind=kOutput, calls=%fused_computation | convolution fusion | flops 7251296256 | bytes 15728640 | tf_op jit(solution)/shard_map/dot_general | solution.py:13
  185.1 0.0 reduce-scatter.2.cloned.1.call-update
  185.2 60.0 %all-reduce.2.cloned.1.call-done = bf16[1152,1024]{1,0:T(8,128)(2,1)} async-done(((bf16[1152,1024]{1,0:T(8,128)(2,1)}), bf16[1152,1024]{1,0:T(8,128)(2,1)}) %all-reduce.2.cloned.1.call-update) | async-done | bytes 2359312 | tf_op jit(solution)/shard_map/psum | solution.py:21
  245.2 4.5 %convert_multiply_fusion = f32[1152,1024]{1,0:T(8,128)} fusion(bf16[1152,1024]{1,0:T(8,128)(2,1)} %all-reduce.2.cloned.1.call-done), kind=kLoop, calls=%fused_computation.1 | loop fusion | flops 2359296 | bytes 7077888 | tf_op jit(solution)/shard_map/mul | solution.py:21
  249.7 121.8 %reduce-scatter.2.cloned.1.call-done = bf16[768,1152]{1,0:T(8,128)(2,1)} async-done(((bf16[3072,1152]{1,0:T(8,128)(2,1)}), bf16[768,1152]{1,0:T(8,128)(2,1)}) %reduce-scatter.2.cloned.1.call-update) | async-done | bytes 1769488 | tf_op jit(solution)/shard_map/reduce_scatter | solution.py:12
Async XLA Ops:
  7.2 165.7 %copy-start = (bf16[1152,1024]{1,0:T(8,128)(2,1)S(1)}, bf16[1152,1024]{1,0:T(8,128)(2,1)}, u32[]{:S(2)}) copy-start(bf16[1152,1024]{1,0:T(8,128)(2,1)} %param.4) | copy-start | bytes 7077892
  7.2 21.9 %all-gather.3.cloned.1.call-start = ((), (), s32[]{:S(2)}) async-start(), calls=%async_computation.1 | async-start | bytes 9437184 | tf_op jit(solution)/shard_map/all_gather | solution.py:9
  7.9 152.1 %all-gather.5.cloned.1.call-start = ((), (), s32[]{:S(2)}) async-start(), calls=%async_computation.3 | async-start | bytes 8847360 | tf_op jit(solution)/shard_map/all_gather | solution.py:8
  8.7 236.5 %all-reduce.2.cloned.1.call-start = ((), (), s32[]{:S(2)}) async-start(), calls=%async_computation.4 | async-start | bytes 4718592 | tf_op jit(solution)/shard_map/psum | solution.py:21
  172.8 198.8 %reduce-scatter.2.cloned.1.call-start = ((), (), s32[]{:S(2)}) async-start(), calls=%async_computation.2 | async-start | bytes 8847360 | tf_op jit(solution)/shard_map/reduce_scatter | solution.py:12
Sparse Core Ops, SparseCore 0:
  9.6 19.4 all-gather.2
  30.6 129.3 all-gather.4
  172.9 72.2 all-reduce.1
  248.0 123.4 reduce-scatter.1
where the time goes:
time: 378 us
  waiting for transfers between devices  335 us (89%)
  matrix products  25 us (7%)
  between operations  13.8 us (4%)
  other arithmetic  4.53 us (1%)
    all_gather x1, waiting for transfers between devices, per_device(): heads_all = lax.all_gather(attn_heads, 'col', axis=0, tiled=True)  131 us
    reduce_scatter x1, waiting for transfers between devices, per_device(): lax.psum_scatter(lax.dot_general(cot_all, out_weight, (((1,), (1,)), ((),...  122 us
    psum x1, waiting for transfers between devices, per_device(): lax.psum(lax.dot_general(heads_all, cot_all, (((0,), (0,)), ((), ())), pr...  60 us
    all_gather x1, waiting for transfers between devices, per_device(): cot_all = lax.all_gather(cotangent, 'row', axis=0, tiled=True)  20.3 us
    dot_general x1, matrix products, per_device(): lax.dot_general(heads_all, cot_all, (((0,), (0,)), ((), ())), preferred_e...  12.7 us
    dot_general x1, matrix products, per_device(): lax.dot_general(cot_all, out_weight, (((1,), (1,)), ((), ())), preferred_...  12.3 us
  transfers between devices with their start and end apart: 4, of which 4 were waited for; matrix products, arithmetic and copies ran while one was open for 4% of the time, Pallas kernels for 0%

commit v1 on v0

v1 whole, which is shorter than its diff:
```python
import functools

import jax
import jax.numpy as jnp
from jax import lax
from jax.experimental import pallas as pl
from jax.experimental.pallas import tpu as pltpu
from jax.sharding import PartitionSpec as P

MESH = pl.DeviceIdType.MESH
TILE = 256


def kernel(n, n_row, n_dp, sum_dp, chunks, heads_ref, weight_ref, cot_ref, head_ref, wg_ref,
           heads_all, cot_all, weight, part, run, acc, wg_send, dp_recv, local_sem,
           z_send, z_recv, row_send, row_recv, rs_send, rs_recv, ag_send, ag_recv):
    c, r, d = lax.axis_index("col"), lax.axis_index("row"), lax.axis_index("dp")
    tok, hq = heads_ref.shape
    wide = hq // chunks
    cot_rows, feat = cot_ref.shape
    piece = wide // n_dp

    barrier = pltpu.get_barrier_semaphore()

    @pl.when(c > 0)
    def _():
        pl.semaphore_signal(barrier, inc=1, device_id={"col": c - 1}, device_id_type=MESH)

    @pl.when(c < n - 1)
    def _():
        pl.semaphore_signal(barrier, inc=1, device_id={"col": c + 1}, device_id_type=MESH)

    for o in range(1, n_row):
        pl.semaphore_signal(barrier, inc=1, device_id={"row": lax.rem(r + o, n_row)}, device_id_type=MESH)
    if sum_dp:
        for o in range(1, n_dp):
            pl.semaphore_signal(barrier, inc=1, device_id={"dp": lax.rem(d + o, n_dp)}, device_id_type=MESH)
    others = (n_row - 1) + (n_dp - 1 if sum_dp else 0)
    pl.semaphore_wait(barrier, others + (c > 0).astype(jnp.int32) + (c < n - 1).astype(jnp.int32))

    def z_copy(way, j, k, src, dst):
        to = jnp.clip(c + 1 - 2 * way, 0, n - 1)
        return pltpu.make_async_remote_copy(
            src_ref=src, dst_ref=dst, send_sem=z_send.at[way, j, k], recv_sem=z_recv.at[way, j, k],
            device_id={"col": to}, device_id_type=MESH)

    def row_copy(o):
        at = pl.ds(pl.multiple_of(r * cot_rows, cot_rows), cot_rows)
        return pltpu.make_async_remote_copy(
            src_ref=cot_ref, dst_ref=cot_all.at[at], send_sem=row_send.at[o], recv_sem=row_recv.at[o],
            device_id={"row": lax.rem(r + o, n_row)}, device_id_type=MESH)

    for o in range(1, n_row):
        row_copy(o).start()
    own_cot = pltpu.make_async_copy(
        cot_ref, cot_all.at[pl.ds(pl.multiple_of(r * cot_rows, cot_rows), cot_rows)], local_sem.at[0])
    own_cot.start()
    own_weight = pltpu.make_async_copy(weight_ref, weight, local_sem.at[1])
    own_weight.start()

    def heads_chunk(k):
        return heads_ref.at[:, pl.ds(k * wide, wide)]

    for k in range(chunks):
        @pl.when(c < n - 1)
        def _():
            z_copy(0, 0, k, heads_chunk(k), heads_all.at[c, k]).start()

        @pl.when(c > 0)
        def _():
            z_copy(1, 0, k, heads_chunk(k), heads_all.at[c, k]).start()

    own_heads = [pltpu.make_async_copy(heads_chunk(k), heads_all.at[c, k], local_sem.at[2 + k])
                 for k in range(chunks)]
    for copy in own_heads:
        copy.start()
    own_weight.wait()
    own_cot.wait()
    for o in range(1, n_row):
        row_copy(o).wait_recv()

    def partials(i, carry):
        t, m = i // (tok // TILE), lax.rem(i, tok // TILE)
        rows = pl.ds(pl.multiple_of(i * TILE, TILE), TILE)
        for k in range(chunks):
            part[t, k, pl.ds(pl.multiple_of(m * TILE, TILE), TILE), :] = lax.dot_general(
                cot_all[rows, :], weight[k * wide:(k + 1) * wide, :], (((1,), (1,)), ((), ())),
                preferred_element_type=jnp.float32).astype(jnp.bfloat16)
        return carry

    lax.fori_loop(0, n * tok // TILE, partials, 0)
    for copy in own_heads:
        copy.wait()

    def add_rows(way, j, k, t):
        def body(m, carry):
            rows = pl.ds(pl.multiple_of(m * TILE, TILE), TILE)
            run[way, j, k, rows, :] = (run[way, j, k, rows, :].astype(jnp.float32)
                                       + part[t, k, rows, :].astype(jnp.float32)).astype(jnp.bfloat16)
            return carry
        lax.fori_loop(0, tok // TILE, body, 0)

    def arrive(way, j, k):
        p = c if way == 0 else n - 1 - c

        def shard(q):
            return q if way == 0 else n - 1 - q

        @pl.when(jnp.logical_and(p > 0, j < p))
        def _():
            s = jnp.clip(shard(p - 1 - j), 0, n - 1)
            z_copy(way, j, k, heads_all.at[s, k], heads_all.at[s, k]).wait_recv()
            if j < n - 1:
                @pl.when(p < n - 1)
                def _():
                    z_copy(way, j + 1, k, heads_all.at[s, k], heads_all.at[s, k]).start()

        @pl.when(jnp.logical_and(p > 0, j >= p))
        def _():
            z_copy(way, j, k, run.at[way, j, k], run.at[way, j, k]).wait_recv()
            if j < n - 1:
                t = jnp.clip(shard(n + p - 1 - j), 0, n - 1)
                add_rows(way, j, k, t)
                z_copy(way, j + 1, k, run.at[way, j, k], run.at[way, j + 1, k]).start()

        if j < n - 1:
            @pl.when(p == 0)
            def _():
                t = shard(n - 1 - j)
                z_copy(way, j + 1, k, part.at[t, k], run.at[way, j + 1, k]).start()

    def weight_chunk(k):
        for s in range(n):
            term = lax.dot_general(
                heads_all[s, k], cot_all[s * tok:(s + 1) * tok, :], (((0,), (0,)), ((), ())),
                preferred_element_type=jnp.float32)
            if s == 0:
                acc[...] = term
            else:
                acc[...] += term
        if not sum_dp:
            wg_ref[pl.ds(pl.multiple_of(k * wide, wide), wide), :] = acc[...].astype(jnp.bfloat16)
            return
        for q in range(n_dp):
            wg_send[k, q] = acc[q * piece:(q + 1) * piece, :].astype(jnp.bfloat16)
        for o in range(1, n_dp):
            to_owner(o, k).start()

    def to_owner(o, k):
        to = lax.rem(d + o, n_dp)
        return pltpu.make_async_remote_copy(
            src_ref=wg_send.at[k, to], dst_ref=dp_recv.at[k, o], send_sem=rs_send.at[o, k],
            recv_sem=rs_recv.at[o, k], device_id={"dp": to}, device_id_type=MESH)

    def piece_at(k, q):
        return pl.ds(pl.multiple_of(k * wide + q * piece, piece), piece)

    def from_owner(o, k):
        return pltpu.make_async_remote_copy(
            src_ref=wg_ref.at[piece_at(k, d)], dst_ref=wg_ref.at[piece_at(k, d)], send_sem=ag_send.at[o, k],
            recv_sem=ag_recv.at[o, k], device_id={"dp": lax.rem(d + o, n_dp)}, device_id_type=MESH)

    def own_piece(k):
        for o in range(1, n_dp):
            to_owner(o, k).wait_recv()
        total = wg_send[k, d].astype(jnp.float32)
        for o in range(1, n_dp):
            total = total + dp_recv[k, o].astype(jnp.float32)
        wg_ref[piece_at(k, d), :] = total.astype(jnp.bfloat16)
        for o in range(1, n_dp):
            from_owner(o, k).start()

    def finish(k):
        def body(m, carry):
            rows = pl.ds(pl.multiple_of(m * TILE, TILE), TILE)
            up = jnp.where(c > 0, run[0, n - 1, k, rows, :].astype(jnp.float32), 0.0)
            down = jnp.where(c < n - 1, run[1, n - 1, k, rows, :].astype(jnp.float32), 0.0)
            total = part[c, k, rows, :].astype(jnp.float32) + up + down
            head_ref[k, rows, :] = total.astype(jnp.bfloat16)
            return carry
        lax.fori_loop(0, tok // TILE, body, 0)

    def clear(way):
        for k in range(chunks):
            run[way, n - 1, k] = jnp.zeros_like(run[way, n - 1, k])

    pl.when(c == 0)(lambda: clear(0))
    pl.when(c == n - 1)(lambda: clear(1))

    for j in range(n):
        def step(k, carry, j=j):
            if j == n - 1 and sum_dp:
                own_piece(k)
            arrive(0, j, k)
            arrive(1, j, k)
            if j == n - 2:
                weight_chunk(k)
            if j == n - 1:
                finish(k)
            return carry
        lax.fori_loop(0, chunks, step, 0)

    def drain(k, carry):
        for j in range(n):
            @pl.when(c < n - 1)
            def _():
                z_copy(0, j, k, run.at[0, j, k], run.at[0, j, k]).wait_send()

            @pl.when(c > 0)
            def _():
                z_copy(1, j, k, run.at[1, j, k], run.at[1, j, k]).wait_send()
        if sum_dp:
            for o in range(1, n_dp):
                to_owner(o, k).wait_send()
                from_owner(o, k).wait_send()
                from_owner(o, k).wait_recv()
        return carry

    lax.fori_loop(0, chunks, drain, 0)
    for o in range(1, n_row):
        row_copy(o).wait_send()


def per_device(sizes, attn_heads, out_weight, cotangent):
    n, n_row, n_dp = sizes["col"], sizes["row"], sizes["dp"]
    tok, hq = attn_heads.shape
    feat = out_weight.shape[1]
    chunks = 3
    wide = hq // chunks
    sum_dp = wide % (16 * n_dp) == 0
    grad_scale = float(tok * n * n_dp) ** (-0.5)
    bf16, dma = jnp.bfloat16, pltpu.SemaphoreType.DMA
    piece = wide // n_dp if sum_dp else 16
    slots = n_dp if sum_dp else 1
    head_grad, weight_sum = pl.pallas_call(
        functools.partial(kernel, n, n_row, n_dp, sum_dp, chunks),
        out_shape=(jax.ShapeDtypeStruct((chunks, tok, wide), bf16), jax.ShapeDtypeStruct((hq, feat), bf16)),
        in_specs=[pl.BlockSpec(memory_space=pl.ANY)] * 3,
        out_specs=[pl.BlockSpec(memory_space=pltpu.VMEM)] * 2,
        scratch_shapes=[
            pltpu.VMEM((n, chunks, tok, wide), bf16),
            pltpu.VMEM((n * tok, feat), bf16),
            pltpu.VMEM((hq, feat), bf16),
            pltpu.VMEM((n, chunks, tok, wide), bf16),
            pltpu.VMEM((2, n, chunks, tok, wide), bf16),
            pltpu.VMEM((wide, feat), jnp.float32),
            pltpu.VMEM((chunks, slots, piece, feat), bf16),
            pltpu.VMEM((chunks, slots, piece, feat), bf16),
            dma((2 + chunks,)),
            dma((2, n, chunks)), dma((2, n, chunks)),
            dma((n_row,)), dma((n_row,)),
            dma((slots, chunks)), dma((slots, chunks)), dma((slots, chunks)), dma((slots, chunks)),
        ],
        compiler_params=pltpu.CompilerParams(
            collective_id=0, has_side_effects=True, vmem_limit_bytes=60 * 1024 * 1024),
        cost_estimate=pl.CostEstimate(
            flops=4 * n * tok * hq * feat, bytes_accessed=4 * n * tok * (hq + feat), transcendentals=0),
    )(attn_heads, out_weight, cotangent)
    head_grad = jnp.concatenate([head_grad[k] for k in range(chunks)], axis=1)
    if not sum_dp:
        weight_sum = lax.psum(weight_sum, "dp")
    return head_grad, weight_sum.astype(jnp.float32) * grad_scale


def solution(mesh):
    return jax.shard_map(
        functools.partial(per_device, dict(mesh.shape)),
        mesh=mesh,
        in_specs=(P(("dp", "col"), "row"), P("row", "col"), P(("dp", "row"), "col")),
        out_specs=(P(("dp", "col"), "row"), P("row", "col")),
        check_vma=False,
    )
```

time: 378 us -> 169 us (0.45)
  waiting for transfers between devices: 335 us -> 0 us
  Pallas kernels: 0 us -> 161 us
  matrix products: 25 us -> 0 us
  between operations: 13.8 us -> 0.65 us
    pallas_call x0 -> x1, Pallas kernels: none -> 161 us  [per_device(): pl.pallas_call(functools.partial(kernel, n, n_row, n_dp, sum_dp, chunks),...]
    all_gather x2 -> x0, waiting for transfers between devices: 151 us -> none  [the longest x1 131 us: per_device(): heads_all = lax.all_gather(attn_heads, 'col', axis=0, tiled=True)]
    reduce_scatter x1 -> x0, waiting for transfers between devices: 122 us -> none  [per_device(): lax.psum_scatter(lax.dot_general(cot_all, out_weight, (((1,), (1,)), ((),...]
    psum x1 -> x0, waiting for transfers between devices: 60 us -> none  [per_device(): lax.psum(lax.dot_general(heads_all, cot_all, (((0,), (0,)), ((), ())), pr...]
    dot_general x2 -> x0, matrix products: 25 us -> none  [the longest x1 12.7 us: per_device(): lax.dot_general(heads_all, cot_all, (((0,), (0,)), ((), ())), preferred_e...]
  transfers between devices with their start and end apart: 4 -> 0, of which waited for: 4 -> 0; matrix products, arithmetic and copies ran while one was open for 4% -> 0% of each run, Pallas kernels for 0% -> 0%
where the time goes in v1:
time: 169 us
  Pallas kernels  161 us (95%)
  other arithmetic  4.21 us (2%)
  local copies, waits for them, and re-layouts  2.54 us (2%)
    pallas_call x1, Pallas kernels, per_device(): pl.pallas_call(functools.partial(kernel, n, n_row, n_dp, sum_dp, chunks),...  161 us

profile of v1, /device:TPU:0, one launch (start us, length us, event | category | flops | bytes accessed | tf_op | source)
XLA Modules:
  0.0 168.5 jit_solution(17960749330272809674)
XLA Ops:
  0.6 161.1 %shard_map.50 = (bf16[3,768,384]{2,1,0:T(8,128)(2,1)}, bf16[1152,1024]{1,0:T(8,128)(2,1)}) custom-call(bf16[768,1152]{1,0:T(8,128)(2,1)} %heads_ref.1, bf16[1152,1024]{1,0:T(8,128)(2,1)} %weight_ref.1, bf16[1536,1024]{1,0:T(8,128)(2,1)} %cot_ref.1), custom_call_target="tpu_custom_call" | custom-call | flops 14495514624 | bytes 26738688 | tf_op jit(solution)/shard_map/pallas_call | solution.py:235
  161.8 1.6 slice_bitcast_fusion.2
  163.4 0.0 copy-start
  163.4 1.4 pad_maximum_fusion
  164.7 0.9 copy-done
  165.7 2.8 %convert_multiply_fusion = f32[1152,1024]{1,0:T(8,128)} fusion(bf16[1152,1024]{1,0:T(8,128)(2,1)S(1)} %copy-done), kind=kLoop, calls=%fused_computation | loop fusion | flops 2359296 | bytes 7077888 | tf_op jit(solution)/shard_map/mul | solution.py:262
Async XLA Ops:
  163.4 2.3 %copy-start = (bf16[1152,1024]{1,0:T(8,128)(2,1)S(1)}, bf16[1152,1024]{1,0:T(8,128)(2,1)}, u32[]{:S(2)}) copy-start(bf16[1152,1024]{1,0:T(8,128)(2,1)} %get-tuple-element.5) | copy-start | bytes 7077892

commit v2 on v1

--- a/solution.py
+++ b/solution.py
@@ -11,8 +11,8 @@
 TILE = 256
 
 
-def kernel(n, n_row, n_dp, sum_dp, chunks, heads_ref, weight_ref, cot_ref, head_ref, wg_ref,
-           heads_all, cot_all, weight, part, run, acc, wg_send, dp_recv, local_sem,
+def kernel(n, n_row, n_dp, sum_dp, chunks, grad_scale, heads_ref, weight_ref, cot_ref, head_ref, wg_ref,
+           heads_all, cot_all, weight, part, run, acc, wg_send, dp_recv, wg_sum, local_sem,
            z_send, z_recv, row_send, row_recv, rs_send, rs_recv, ag_send, ag_recv):
     c, r, d = lax.axis_index("col"), lax.axis_index("row"), lax.axis_index("dp")
     tok, hq = heads_ref.shape
@@ -152,12 +152,9 @@
             src_ref=wg_send.at[k, to], dst_ref=dp_recv.at[k, o], send_sem=rs_send.at[o, k],
             recv_sem=rs_recv.at[o, k], device_id={"dp": to}, device_id_type=MESH)
 
-    def piece_at(k, q):
-        return pl.ds(pl.multiple_of(k * wide + q * piece, piece), piece)
-
     def from_owner(o, k):
         return pltpu.make_async_remote_copy(
-            src_ref=wg_ref.at[piece_at(k, d)], dst_ref=wg_ref.at[piece_at(k, d)], send_sem=ag_send.at[o, k],
+            src_ref=wg_sum.at[k, d], dst_ref=wg_sum.at[k, d], send_sem=ag_send.at[o, k],
             recv_sem=ag_recv.at[o, k], device_id={"dp": lax.rem(d + o, n_dp)}, device_id_type=MESH)
 
     def own_piece(k):
@@ -166,9 +163,16 @@
         total = wg_send[k, d].astype(jnp.float32)
         for o in range(1, n_dp):
             total = total + dp_recv[k, o].astype(jnp.float32)
-        wg_ref[piece_at(k, d), :] = total.astype(jnp.bfloat16)
+        wg_sum[k, d] = total.astype(jnp.bfloat16)
         for o in range(1, n_dp):
             from_owner(o, k).start()
+
+    def widen(k):
+        for o in range(1, n_dp):
+            from_owner(o, k).wait_recv()
+        for q in range(n_dp):
+            at = k * wide + q * piece
+            wg_ref[at:at + piece, :] = wg_sum[k, q].astype(jnp.float32) * grad_scale
 
     def finish(k):
         def body(m, carry):
@@ -176,7 +180,7 @@
             up = jnp.where(c > 0, run[0, n - 1, k, rows, :].astype(jnp.float32), 0.0)
             down = jnp.where(c < n - 1, run[1, n - 1, k, rows, :].astype(jnp.float32), 0.0)
             total = part[c, k, rows, :].astype(jnp.float32) + up + down
-            head_ref[k, rows, :] = total.astype(jnp.bfloat16)
+            head_ref[rows, pl.ds(k * wide, wide)] = total.astype(jnp.bfloat16)
             return carry
         lax.fori_loop(0, tok // TILE, body, 0)
 
@@ -187,18 +191,26 @@
     pl.when(c == 0)(lambda: clear(0))
     pl.when(c == n - 1)(lambda: clear(1))
 
-    for j in range(n):
+    for j in range(n - 1):
         def step(k, carry, j=j):
-            if j == n - 1 and sum_dp:
-                own_piece(k)
             arrive(0, j, k)
             arrive(1, j, k)
             if j == n - 2:
                 weight_chunk(k)
-            if j == n - 1:
-                finish(k)
             return carry
         lax.fori_loop(0, chunks, step, 0)
+
+    for k in range(chunks):
+        if sum_dp:
+            for late in range(chunks):
+                if max(late - 1, 0) == k:
+                    own_piece(late)
+            if k == chunks - 1:
+                for late in range(chunks):
+                    widen(late)
+        arrive(0, n - 1, k)
+        arrive(1, n - 1, k)
+        finish(k)
 
     def drain(k, carry):
         for j in range(n):
@@ -213,7 +225,6 @@
             for o in range(1, n_dp):
                 to_owner(o, k).wait_send()
                 from_owner(o, k).wait_send()
-                from_owner(o, k).wait_recv()
         return carry
 
     lax.fori_loop(0, chunks, drain, 0)
@@ -233,8 +244,8 @@
     piece = wide // n_dp if sum_dp else 16
     slots = n_dp if sum_dp else 1
     head_grad, weight_sum = pl.pallas_call(
-        functools.partial(kernel, n, n_row, n_dp, sum_dp, chunks),
-        out_shape=(jax.ShapeDtypeStruct((chunks, tok, wide), bf16), jax.ShapeDtypeStruct((hq, feat), bf16)),
+        functools.partial(kernel, n, n_row, n_dp, sum_dp, chunks, grad_scale),
+        out_shape=(pltpu.VMEM((tok, hq), bf16), pltpu.VMEM((hq, feat), jnp.float32 if sum_dp else bf16)),
         in_specs=[pl.BlockSpec(memory_space=pl.ANY)] * 3,
         out_specs=[pl.BlockSpec(memory_space=pltpu.VMEM)] * 2,
         scratch_shapes=[
@@ -246,20 +257,20 @@
             pltpu.VMEM((wide, feat), jnp.float32),
             pltpu.VMEM((chunks, slots, piece, feat), bf16),
             pltpu.VMEM((chunks, slots, piece, feat), bf16),
+            pltpu.VMEM((chunks, slots, piece, feat), bf16),
             dma((2 + chunks,)),
             dma((2, n, chunks)), dma((2, n, chunks)),
             dma((n_row,)), dma((n_row,)),
             dma((slots, chunks)), dma((slots, chunks)), dma((slots, chunks)), dma((slots, chunks)),
         ],
         compiler_params=pltpu.CompilerParams(
-            collective_id=0, has_side_effects=True, vmem_limit_bytes=60 * 1024 * 1024),
+            collective_id=0, has_side_effects=True, vmem_limit_bytes=54 * 1024 * 1024),
         cost_estimate=pl.CostEstimate(
             flops=4 * n * tok * hq * feat, bytes_accessed=4 * n * tok * (hq + feat), transcendentals=0),
     )(attn_heads, out_weight, cotangent)
-    head_grad = jnp.concatenate([head_grad[k] for k in range(chunks)], axis=1)
     if not sum_dp:
-        weight_sum = lax.psum(weight_sum, "dp")
-    return head_grad, weight_sum.astype(jnp.float32) * grad_scale
+        weight_sum = lax.psum(weight_sum, "dp").astype(jnp.float32) * grad_scale
+    return head_grad, weight_sum
 
 
 def solution(mesh):

time: 169 us -> 163 us (0.964)
  other arithmetic: 4.21 us -> 0 us
  Pallas kernels: 161 us -> 159 us
    mul x1 -> x0, other arithmetic: 2.85 us -> none  [per_device(): return (head_grad, weight_sum.astype(jnp.float32) * grad_scale)]
    unnamed x2, local copies, waits for them, and re-layouts: 0.94 us -> 3.39 us
    pallas_call x1, Pallas kernels: 161 us -> 159 us  [per_device(): pl.pallas_call(functools.partial(kernel, n, n_row, n_dp, sum_dp, chunks,...]
where the time goes in v2:
time: 163 us
  Pallas kernels  159 us (98%)
  local copies, waits for them, and re-layouts  3.39 us (2%)
    pallas_call x1, Pallas kernels, per_device(): pl.pallas_call(functools.partial(kernel, n, n_row, n_dp, sum_dp, chunks,...  159 us
    unnamed x2, local copies, waits for them, and re-layouts  3.39 us

profile of v2, /device:TPU:0, one launch (start us, length us, event | category | flops | bytes accessed | tf_op | source)
XLA Modules:
  0.0 163.2 jit_solution(9012710371785668847)
XLA Ops:
  0.6 159.2 %shard_map.50 = (bf16[768,1152]{1,0:T(8,128)(2,1)S(1)}, f32[1152,1024]{1,0:T(8,128)S(1)}) custom-call(bf16[768,1152]{1,0:T(8,128)(2,1)} %heads_ref.1, bf16[1152,1024]{1,0:T(8,128)(2,1)} %weight_ref.1, bf16[1536,1024]{1,0:T(8,128)(2,1)} %cot_ref.1), custom_call_target="tpu_custom_call" | custom-call | flops 14495514624 | bytes 26738688 | tf_op jit(solution)/shard_map/pallas_call | solution.py:246
  159.8 1.2 copy.7
  161.0 2.2 %copy.8 = f32[1152,1024]{1,0:T(8,128)} copy(f32[1152,1024]{1,0:T(8,128)S(1)} %get-tuple-element.3) | data formatting | bytes 9437184

commit v3 on v2

--- a/solution.py
+++ b/solution.py
@@ -50,6 +50,18 @@
             src_ref=cot_ref, dst_ref=cot_all.at[at], send_sem=row_send.at[o], recv_sem=row_recv.at[o],
             device_id={"row": lax.rem(r + o, n_row)}, device_id_type=MESH)
 
+    def heads_chunk(k):
+        return heads_ref.at[:, pl.ds(k * wide, wide)]
+
+    for k in range(chunks):
+        @pl.when(c < n - 1)
+        def _():
+            z_copy(0, 0, k, heads_chunk(k), heads_all.at[c, k]).start()
+
+        @pl.when(c > 0)
+        def _():
+            z_copy(1, 0, k, heads_chunk(k), heads_all.at[c, k]).start()
+
     for o in range(1, n_row):
         row_copy(o).start()
     own_cot = pltpu.make_async_copy(
@@ -57,18 +69,6 @@
     own_cot.start()
     own_weight = pltpu.make_async_copy(weight_ref, weight, local_sem.at[1])
     own_weight.start()
-
-    def heads_chunk(k):
-        return heads_ref.at[:, pl.ds(k * wide, wide)]
-
-    for k in range(chunks):
-        @pl.when(c < n - 1)
-        def _():
-            z_copy(0, 0, k, heads_chunk(k), heads_all.at[c, k]).start()
-
-        @pl.when(c > 0)
-        def _():
-            z_copy(1, 0, k, heads_chunk(k), heads_all.at[c, k]).start()
 
     own_heads = [pltpu.make_async_copy(heads_chunk(k), heads_all.at[c, k], local_sem.at[2 + k])
                  for k in range(chunks)]
@@ -200,6 +200,24 @@
             return carry
         lax.fori_loop(0, chunks, step, 0)
 
+    def sent(j, k):
+        @pl.when(c < n - 1)
+        def _():
+            z_copy(0, j, k, run.at[0, j, k], run.at[0, j, k]).wait_send()
+
+        @pl.when(c > 0)
+        def _():
+            z_copy(1, j, k, run.at[1, j, k], run.at[1, j, k]).wait_send()
+
+    def drain(k, carry):
+        for j in range(n - 1):
+            sent(j, k)
+        if sum_dp:
+            for o in range(1, n_dp):
+                to_owner(o, k).wait_send()
+                from_owner(o, k).wait_send()
+        return carry
+
     for k in range(chunks):
         if sum_dp:
             for late in range(chunks):
@@ -208,28 +226,27 @@
             if k == chunks - 1:
                 for late in range(chunks):
                     widen(late)
+        if k == chunks - 1:
+            lax.fori_loop(0, chunks, drain, 0)
+            for o in range(1, n_row):
+                row_copy(o).wait_send()
         arrive(0, n - 1, k)
         arrive(1, n - 1, k)
         finish(k)
-
-    def drain(k, carry):
-        for j in range(n):
-            @pl.when(c < n - 1)
-            def _():
-                z_copy(0, j, k, run.at[0, j, k], run.at[0, j, k]).wait_send()
-
-            @pl.when(c > 0)
-            def _():
-                z_copy(1, j, k, run.at[1, j, k], run.at[1, j, k]).wait_send()
-        if sum_dp:
-            for o in range(1, n_dp):
-                to_owner(o, k).wait_send()
-                from_owner(o, k).wait_send()
-        return carry
-
-    lax.fori_loop(0, chunks, drain, 0)
-    for o in range(1, n_row):
-        row_copy(o).wait_send()
+    for k in range(chunks):
+        sent(n - 1, k)
+
+
+def store(head_ref, wg_ref, head_out, wg_out, sem):
+    copies = [pltpu.make_async_copy(head_ref, head_out, sem.at[0])]
+    half = wg_ref.shape[0] // 2
+    for i in range(2):
+        rows = pl.ds(i * half, half)
+        copies.append(pltpu.make_async_copy(wg_ref.at[rows], wg_out.at[rows], sem.at[1 + i]))
+    for copy in copies:
+        copy.start()
+    for copy in copies:
+        copy.wait()
 
 
 def per_device(sizes, attn_heads, out_weight, cotangent):
@@ -270,7 +287,15 @@
     )(attn_heads, out_weight, cotangent)
     if not sum_dp:
         weight_sum = lax.psum(weight_sum, "dp").astype(jnp.float32) * grad_scale
-    return head_grad, weight_sum
+        return head_grad, weight_sum
+    return pl.pallas_call(
+        store,
+        out_shape=(jax.ShapeDtypeStruct((tok, hq), bf16), jax.ShapeDtypeStruct((hq, feat), jnp.float32)),
+        in_specs=[pl.BlockSpec(memory_space=pltpu.VMEM)] * 2,
+        out_specs=[pl.BlockSpec(memory_space=pl.ANY)] * 2,
+        scratch_shapes=[dma((3,))],
+        compiler_params=pltpu.CompilerParams(vmem_limit_bytes=16 * 1024 * 1024),
+    )(head_grad, weight_sum)
 
 
 def solution(mesh):

time: 163 us -> 163 us (level)
  local copies, waits for them, and re-layouts: 3.39 us -> 0 us
  Pallas kernels: 159 us -> 162 us
    unnamed x2 -> x0, local copies, waits for them, and re-layouts: 3.39 us -> none
    pallas_call x0 -> x1, Pallas kernels: none -> 2.79 us  [per_device(): pl.pallas_call(store, out_shape=(jax.ShapeDtypeStruct((tok, hq), bf16), j...]
where the time goes in v3:
time: 163 us
  Pallas kernels  162 us (99%)
    pallas_call x1, Pallas kernels, per_device(): pl.pallas_call(functools.partial(kernel, n, n_row, n_dp, sum_dp, chunks,...  159 us

profile of v3, /device:TPU:0, one launch (start us, length us, event | category | flops | bytes accessed | tf_op | source)
XLA Modules:
  0.0 162.5 jit_solution(12121324519355606015)
XLA Ops:
  0.6 159.1 %shard_map.50 = (bf16[768,1152]{1,0:T(8,128)(2,1)S(1)}, f32[1152,1024]{1,0:T(8,128)S(1)}) custom-call(bf16[768,1152]{1,0:T(8,128)(2,1)} %heads_ref.1, bf16[1152,1024]{1,0:T(8,128)(2,1)} %weight_ref.1, bf16[1536,1024]{1,0:T(8,128)(2,1)} %cot_ref.1), custom_call_target="tpu_custom_call" | custom-call | flops 14495514624 | bytes 26738688 | tf_op jit(solution)/shard_map/pallas_call | solution.py:263
  159.8 2.8 %shard_map.51 = (bf16[768,1152]{1,0:T(8,128)(2,1)}, f32[1152,1024]{1,0:T(8,128)}) custom-call(bf16[768,1152]{1,0:T(8,128)(2,1)S(1)} %get-tuple-element.4.head_ref, f32[1152,1024]{1,0:T(8,128)S(1)} %get-tuple-element.5.wg_ref), custom_call_target="tpu_custom_call" | custom-call | tf_op jit(solution)/shard_map/pallas_call | solution.py:291

commit v4 on v3

--- a/solution.py
+++ b/solution.py
@@ -253,7 +253,7 @@
     n, n_row, n_dp = sizes["col"], sizes["row"], sizes["dp"]
     tok, hq = attn_heads.shape
     feat = out_weight.shape[1]
-    chunks = 3
+    chunks = hq // 128
     wide = hq // chunks
     sum_dp = wide % (16 * n_dp) == 0
     grad_scale = float(tok * n * n_dp) ** (-0.5)

time: 163 us -> 164 us (level)
  no operation moved by 1% of the time
where the time goes in v4:
time: 164 us
  Pallas kernels  163 us (99%)
    pallas_call x1, Pallas kernels, per_device(): pl.pallas_call(functools.partial(kernel, n, n_row, n_dp, sum_dp, chunks,...  161 us

profile of v4, /device:TPU:0, one launch (start us, length us, event | category | flops | bytes accessed | tf_op | source)
XLA Modules:
  0.0 164.1 jit_solution(16966844191967464118)
XLA Ops:
  0.6 160.7 %shard_map.50 = (bf16[768,1152]{1,0:T(8,128)(2,1)S(1)}, f32[1152,1024]{1,0:T(8,128)S(1)}) custom-call(bf16[768,1152]{1,0:T(8,128)(2,1)} %heads_ref.1, bf16[1152,1024]{1,0:T(8,128)(2,1)} %weight_ref.1, bf16[1536,1024]{1,0:T(8,128)(2,1)} %cot_ref.1), custom_call_target="tpu_custom_call" | custom-call | flops 14495514624 | bytes 26738688 | tf_op jit(solution)/shard_map/pallas_call | solution.py:263
  161.3 2.8 %shard_map.51 = (bf16[768,1152]{1,0:T(8,128)(2,1)}, f32[1152,1024]{1,0:T(8,128)}) custom-call(bf16[768,1152]{1,0:T(8,128)(2,1)S(1)} %get-tuple-element.4.head_ref, f32[1152,1024]{1,0:T(8,128)S(1)} %get-tuple-element.5.wg_ref), custom_call_target="tpu_custom_call" | custom-call | tf_op jit(solution)/shard_map/pallas_call | solution.py:291
